TPU v7x, 32 devices: a whole 2x2x4 slice. The times are simulated.
32 devices in a mesh: row: 8 (over y, x, core), col: 4 (over z).
Axes of the slice: x: 2, y: 2, z: 4, core: 2. Of those that a mesh axis runs over, the one named last changes fastest.
Arguments:
- noisy: float32 [2048, 4096], P('row', 'col'), may hold values from -6 to 6
- strength: float32 [2048, 4096], P('row', 'col'), may hold values from 0.1 to 1
Outputs:
- denoised: float32 [2048, 4096], P('row', 'col')
- dual: float32 [2, 2048, 4096], P(None, 'row', 'col')
All inputs are finite; a program needn't handle non-finite values.
Results may differ from a plain program's by a relative error of at most 0.0003.
Values sent between devices are 32-bit elements; how exact they have to be, the bound alone decides.
A program may use at most 128 MiB of HBM per device.

v0:
```python
from functools import partial

import jax
import jax.numpy as jnp
from jax import lax
from jax.experimental import pallas as pl
from jax.experimental.pallas import tpu as pltpu
from jax.sharding import PartitionSpec as P

F32 = jnp.float32
BF16 = jnp.bfloat16
MESH = pl.DeviceIdType.MESH
VMEM = pltpu.VMEM

damping = 0.01
GUARD = 8
HALO0 = 8
HALO1 = 72
DIRECTIONS = ((-1, 0), (1, 0), (0, -1), (0, 1), (-1, -1), (-1, 1), (1, -1), (1, 1))
VMEM_LIMIT = 58 * 1024 * 1024


def centre(level):
    return 4.0 + damping * 4.0**level


def iota(shape, dim):
    return lax.broadcasted_iota(jnp.int32, shape, dim)


def west(x):
    return pltpu.roll(x, 1, 1)


def east(x):
    return pltpu.roll(x, x.shape[1] - 1, 1)


def north(x):
    return pltpu.roll(x, 1, 0)


def south(x):
    return pltpu.roll(x, x.shape[0] - 1, 0)


def split(x):
    high = x.astype(BF16)
    return high, (x - high.astype(F32)).astype(BF16)


def times(x, matrix):
    high, low = split(x)
    return jnp.dot(high, matrix, preferred_element_type=F32) + jnp.dot(
        low, matrix, preferred_element_type=F32
    )


def apply_rows(matrix, x):
    high, low = split(x)
    return jnp.dot(matrix, high, preferred_element_type=F32) + jnp.dot(
        matrix, low, preferred_element_type=F32
    )


def as_matrix(mask):
    return jnp.where(mask, 1.0, 0.0).astype(BF16)


def pair_rows(coarse, fine):
    return as_matrix((iota((coarse, fine), 1) >> 1) == iota((coarse, fine), 0))


def pair_cols():
    return as_matrix((iota((256, 128), 0) >> 1) == iota((256, 128), 1))


def pair_cols_tail():
    i = iota((128, 128), 0)
    return as_matrix((i >> 1) + jnp.where(i >= 64, 64, 0) == iota((128, 128), 1))


def interleave():
    i = iota((256, 256), 0)
    return as_matrix(2 * (i & 127) + (i >> 7) == iota((256, 256), 1))


def interleave_tail():
    i = iota((256, 128), 0)
    n = iota((256, 128), 1)
    return as_matrix(2 * (i & 127) + (i >> 7) == n + jnp.where(n >= 64, 128, 0))


def spread_rows(fine, coarse, offset):
    f = iota((fine, coarse), 0)
    k = iota((fine, coarse), 1)
    near = (f >> 1) + offset
    far = near + 2 * (f & 1) - 1
    return (jnp.where(k == near, 0.75, 0.0) + jnp.where(k == far, 0.25, 0.0)).astype(BF16)


def spread_cols(c):
    return 0.75 * c + 0.25 * west(c), 0.75 * c + 0.25 * east(c)


def joined(even, odd, block):
    at = slice(128 * block, 128 * block + 128)
    return jnp.concatenate([even[:, at], odd[:, at]], axis=1)


def col_index(width, own, right):
    lane = iota((1, width), 1)
    return lax.axis_index("col") * own + jnp.where(lane < own + right, lane, lane - width)


def col_inside(width, own, right):
    g = col_index(width, own, right)
    return (g >= 0) & (g < own * lax.axis_size("col"))


def row_inside(count, own, halo):
    g = lax.axis_index("row") * own - halo + iota((count, 1), 0)
    return (g >= 0) & (g < own * lax.axis_size("row"))


def weights(level, count, width, own_rows, own_cols, halo, right):
    inside = row_inside(count, own_rows, halo) & col_inside(width, own_cols, right)
    return jnp.where(inside, 0.8 / centre(level), 0.0)


def neighbour_exists(drow, dcol):
    row = lax.axis_index("row") + drow
    col = lax.axis_index("col") + dcol
    return (
        (row >= 0) & (row < lax.axis_size("row")) & (col >= 0) & (col < lax.axis_size("col"))
    )


def exchange(sources, targets, send_sem, recv_sem):
    barrier = pltpu.get_barrier_semaphore()
    row, col = lax.axis_index("row"), lax.axis_index("col")
    for drow, dcol in DIRECTIONS:

        @pl.when(neighbour_exists(drow, dcol))
        def _():
            pl.semaphore_signal(
                barrier, inc=1, device_id=(row + drow, col + dcol), device_id_type=MESH
            )

    pl.semaphore_wait(
        barrier, sum(jnp.where(neighbour_exists(*d), 1, 0) for d in DIRECTIONS)
    )

    def copy(d):
        drow, dcol = DIRECTIONS[d]
        return pltpu.make_async_remote_copy(
            src_ref=sources[d],
            dst_ref=targets[d],
            send_sem=send_sem.at[d],
            recv_sem=recv_sem.at[d],
            device_id=(row + drow, col + dcol),
            device_id_type=MESH,
        )

    order = (2, 3, 4, 5, 6, 7, 0, 1)
    for d in order:

        @pl.when(neighbour_exists(*DIRECTIONS[d]))
        def _():
            copy(d).start()

    for d in order:
        drow, dcol = DIRECTIONS[d]

        @pl.when(neighbour_exists(drow, dcol))
        def _():
            copy(d).wait_send()

        @pl.when(neighbour_exists(-drow, -dcol))
        def _():
            copy(d).wait_recv()


def exchange_image(
    noisy, strength, *rest
):
    targets, scratch = rest[:8], rest[8:]
    vertical, sides, corners, send_sem, recv_sem = scratch
    rows, cols = noisy.shape
    lane = iota((16, 128), 1)
    for k, ref in enumerate((noisy, strength)):
        at = slice(8 * k, 8 * k + 8)
        vertical[0, at] = ref[0:8, :]
        vertical[1, at] = ref[rows - 8 : rows, :]
        corners[0, at] = ref[0:8, 0:128]
        corners[1, at] = ref[0:8, cols - 128 : cols]
        corners[2, at] = ref[rows - 8 : rows, 0:128]
        corners[3, at] = ref[rows - 8 : rows, cols - 128 : cols]
        first = jnp.zeros((16, 128), F32)
        last = jnp.zeros((16, 128), F32)
        for g in range(16):
            here = (lane >= 8 * g) & (lane < 8 * g + 8)
            near = slice(16 * g, 16 * g + 16)
            first = jnp.where(here, pltpu.roll(ref[near, 0:128], 8 * g, 1), first)
            last = jnp.where(
                here, pltpu.roll(ref[near, cols - 128 : cols], (8 * g + 8) % 128, 1), last
            )
        sides[0, 16 * k : 16 * k + 16] = first
        sides[1, 16 * k : 16 * k + 16] = last
    sources = (
        vertical.at[0],
        vertical.at[1],
        sides.at[0],
        sides.at[1],
        corners.at[0],
        corners.at[1],
        corners.at[2],
        corners.at[3],
    )
    exchange(sources, targets, send_sem, recv_sem)


def exchange_source(source, *rest):
    targets, (send_sem, recv_sem) = rest[:8], rest[8:]
    rows, cols = source.shape
    up, down = pl.ds(0, HALO1), pl.ds(rows - HALO1, HALO1)
    left, right = pl.ds(0, 128), pl.ds(cols - 128, 128)
    sources = (
        source.at[up, :],
        source.at[down, :],
        source.at[:, left],
        source.at[:, right],
        source.at[up, left],
        source.at[up, right],
        source.at[down, left],
        source.at[down, right],
    )
    exchange(sources, targets, send_sem, recv_sem)


def tile_valid(tile, own, halo):
    g = lax.axis_index("row") * own - halo + tile * 8
    return jnp.where((g >= 0) & (g < own * lax.axis_size("row")), 1.0, 0.0)


def neighbours(ref, start):
    x = ref[pl.ds(start, 24), :]
    middle = x[8:16]
    return middle, (x[7:15] + x[9:17]) + (west(middle) + east(middle))


def for_tiles(first, last, body, unroll=2):
    def step(tile, carry):
        body(tile, pl.multiple_of(tile * 8, 8))
        return carry

    lax.fori_loop(first, last, step, 0, unroll=unroll)


def sweep(old, new, source, gain, own, halo, tiles):
    def body(tile, start):
        middle, beside = neighbours(old, start)
        k = gain * tile_valid(tile, own, halo)
        new[pl.ds(start + 8, 8), :] = 0.2 * middle + k * (source[pl.ds(start + 8, 8), :] + beside)

    for_tiles(0, tiles, body)


def first_sweep(new, source, gain, own, halo, tiles):
    def body(tile, start):
        k = gain * tile_valid(tile, own, halo)
        new[pl.ds(start + 8, 8), :] = k * source[pl.ds(start + 8, 8), :]

    for_tiles(0, tiles, body)


def dual_masks(tile, own_rows, width, own_cols, halo, right):
    g = lax.axis_index("row") * own_rows - halo + tile * 8 + iota((8, 1), 0)
    return jnp.where((g >= 0) & (g < own_rows * lax.axis_size("row") - 1), 1.0, 0.0)


def shrunk(qa, qb, bound):
    shrink = jnp.minimum(1.0, bound * lax.rsqrt(qa * qa + qb * qb))
    return qa * shrink, qb * shrink


def clear_guards(ref):
    rows, width = ref.shape
    ref[0:GUARD, :] = jnp.zeros((GUARD, width), ref.dtype)
    ref[rows - GUARD : rows, :] = jnp.zeros((GUARD, width), ref.dtype)


def half_cols_mask(width, own, right):
    g = col_index(width, own, right)
    return jnp.where((g >= 0) & (g < own * lax.axis_size("col") - 1), 0.5, 0.0)


def down_level0(
    noisy, strength, up, down, left, right, upleft, upright, downleft, downright,
    wide_noisy, wide_strength, dual_a, dual_b, source, values, coarse, other,
):
    rows, cols = noisy.shape
    width = wide_noisy.shape[1]
    total = wide_noisy.shape[0]
    tiles = (total - 2 * GUARD) // 8
    lane = iota((16, 128), 1)
    right_end = jnp.where(neighbour_exists(0, 1), 8, 0)
    left_start = jnp.where(neighbour_exists(0, -1), 120, 128)
    top = GUARD + HALO0
    for k, (ref, wide, fill) in enumerate(((noisy, wide_noisy, 0.0), (strength, wide_strength, 1.0))):
        wide[top : top + rows, 0:cols] = ref[...]
        wide[0:top, :] = jnp.full((top, width), fill, F32)
        wide[top + rows : total, :] = jnp.full((total - top - rows, width), fill, F32)
        from_right = right[16 * k : 16 * k + 16]
        from_left = left[16 * k : 16 * k + 16]
        for g in range(16):
            piece = jnp.where(
                lane < right_end,
                pltpu.roll(from_right, (128 - 8 * g) % 128, 1),
                jnp.where(lane >= left_start, pltpu.roll(from_left, (120 - 8 * g) % 128, 1), fill),
            )
            wide[top + 16 * g : top + 16 * g + 16, cols:width] = piece
        at = slice(8 * k, 8 * k + 8)
        lane8 = lane[0:8]
        for edge, other_left, other_right, drow, place in (
            (up, upleft, upright, -1, GUARD),
            (down, downleft, downright, 1, top + rows),
        ):

            @pl.when(neighbour_exists(drow, 0))
            def _():
                wide[place : place + 8, 0:cols] = edge[at, :]
                wide[place : place + 8, cols:width] = jnp.where(
                    lane8 < right_end,
                    other_right[at, :],
                    jnp.where(lane8 >= left_start, other_left[at, :], fill),
                )

    for ref in (dual_a, dual_b, source, values, other):
        clear_guards(ref)

    inside = col_inside(width, cols, 64)
    gain = jnp.where(inside, 0.8 / centre(0), 0.0)
    half_cols = half_cols_mask(width, cols, 64)

    def first_step(tile, start):
        x = wide_noisy[pl.ds(start + 8, 16), :]
        w = x[0:8]
        half_rows = 0.5 * dual_masks(tile, rows, width, cols, HALO0, 64)
        qa = half_rows * (x[1:9] - w)
        qb = half_cols * (east(w) - w)
        a, b = shrunk(qa, qb, wide_strength[pl.ds(start + 8, 8), :])
        dual_a[pl.ds(start + 8, 8), :] = a
        dual_b[pl.ds(start + 8, 8), :] = b
        above = dual_a[pl.ds(start, 16), :][7:15]
        s = 0.8 * ((a - above) + (b - west(b)))
        source[pl.ds(start + 8, 8), :] = s
        other[pl.ds(start + 8, 8), :] = (gain * tile_valid(tile, rows, HALO0)) * s

    for_tiles(0, tiles, first_step, unroll=1)
    sweep(other, values, source, gain, rows, HALO0, tiles)
    sweep(values, other, source, gain, rows, HALO0, tiles)

    def residual(tile, start):
        middle, beside = neighbours(other, start)
        values[pl.ds(start + 8, 8), :] = (
            source[pl.ds(start + 8, 8), :] - centre(0) * middle + beside
        )

    for_tiles(1, tiles - 1, residual)
    rows_matrix = pair_rows(rows // 2, rows)
    cols_matrix = pair_cols()
    for block in range(cols // 256):
        piece = values[top : top + rows, 256 * block : 256 * block + 256]
        coarse[:, 128 * block : 128 * block + 128] = times(
            apply_rows(rows_matrix, piece), cols_matrix
        )

    def back(tile, start):
        values[pl.ds(start + 8, 8), :] = other[pl.ds(start + 8, 8), :]

    for_tiles(0, tiles, back)


def relax(e, source, gain):
    beside = (north(e) + south(e)) + (west(e) + east(e))
    return 0.2 * e + gain * (source + beside)


def smoothed(source, gain):
    e = gain * source
    e = relax(e, source, gain)
    return relax(e, source, gain)


def remaining(e, source, level):
    return source - centre(level) * e + ((north(e) + south(e)) + (west(e) + east(e)))


def coarse_levels(source2, own_rows, own_cols):
    n2, n3, n4 = 144, 80, 48
    gain2 = weights(2, n2, own_cols + 128, own_rows, own_cols, 36, 64)
    gain3 = weights(3, n3, 256, own_rows // 2, own_cols // 2, 18, 64)
    gain4 = weights(4, n4, 128, own_rows // 4, own_cols // 4, 9, 32)
    spread, spread_tail = interleave(), interleave_tail()
    pairs, pairs_tail = pair_cols(), pair_cols_tail()

    e2 = smoothed(source2, gain2)
    left = apply_rows(pair_rows(n3, n2), remaining(e2, source2, 2))
    source3 = jnp.concatenate(
        [times(left[:, 0:256], pairs), times(left[:, 256:384], pairs_tail)], axis=1
    )
    e3 = smoothed(source3, gain3)
    source4 = times(apply_rows(pair_rows(n4, n3), remaining(e3, source3, 3)), pairs)
    e4 = smoothed(source4, gain4)

    even, odd = spread_cols(e4)
    wide = times(joined(even, odd, 0), spread)
    e3 = e3 + apply_rows(spread_rows(n3, n4, 0), wide)
    e3 = jnp.where(gain3 > 0.0, e3, 0.0)
    for _ in range(3):
        e3 = relax(e3, source3, gain3)

    even, odd = spread_cols(e3)
    wide = jnp.concatenate(
        [times(joined(even, odd, 0), spread), times(joined(even, odd, 1), spread_tail)], axis=1
    )
    e2 = e2 + apply_rows(spread_rows(n2, n3, 0), wide)
    e2 = jnp.where(gain2 > 0.0, e2, 0.0)
    for _ in range(3):
        e2 = relax(e2, source2, gain2)
    return e2


def up_levels(
    coarse, up, down, left, right, upleft, upright, downleft, downright,
    wide_noisy, wide_strength, dual_a, dual_b, source, values,
    image, dual,
    source1, one, two, other, new_a,
):
    rows1, cols1 = coarse.shape
    width1 = cols1 + 256
    tiles1 = (source1.shape[0] - 2 * GUARD) // 8
    top1 = GUARD + HALO1
    source1[...] = jnp.zeros(source1.shape, F32)
    for ref in (one, two, other, new_a):
        clear_guards(ref)
    source1[top1 : top1 + rows1, 0:cols1] = coarse[...]
    above = slice(GUARD, top1)
    beside = slice(top1, top1 + rows1)
    below = slice(top1 + rows1, top1 + rows1 + HALO1)
    own = slice(0, cols1)
    to_right = slice(cols1, cols1 + 128)
    to_left = slice(cols1 + 128, width1)
    for ref, drow, dcol, at_rows, at_cols in (
        (up, -1, 0, above, own),
        (down, 1, 0, below, own),
        (left, 0, -1, beside, to_left),
        (right, 0, 1, beside, to_right),
        (upleft, -1, -1, above, to_left),
        (upright, -1, 1, above, to_right),
        (downleft, 1, -1, below, to_left),
        (downright, 1, 1, below, to_right),
    ):

        @pl.when(neighbour_exists(drow, dcol))
        def _():
            source1[at_rows, at_cols] = ref[...]

    inside1 = col_inside(width1, cols1, 128)
    gain1 = jnp.where(inside1, 0.8 / centre(1), 0.0)
    first_sweep(one, source1, gain1, rows1, HALO1, tiles1)
    sweep(one, two, source1, gain1, rows1, HALO1, tiles1)
    sweep(two, one, source1, gain1, rows1, HALO1, tiles1)

    def residual(tile, start):
        middle, near = neighbours(one, start)
        two[pl.ds(start + 8, 8), :] = source1[pl.ds(start + 8, 8), :] - centre(1) * middle + near

    for_tiles(0, tiles1, residual)
    count1 = 8 * tiles1
    body1 = slice(GUARD, GUARD + count1)
    rows_matrix = pair_rows(144, count1)
    pairs = pair_cols()
    source2 = jnp.concatenate(
        [
            times(apply_rows(rows_matrix, two[body1, 256 * k : 256 * k + 256]), pairs)
            for k in range(width1 // 256)
        ],
        axis=1,
    )
    e2 = coarse_levels(source2, rows1 // 2, cols1 // 2)

    spread, spread_tail = interleave(), interleave_tail()
    matrix = spread_rows(count1, 144, 0)
    even, odd = spread_cols(e2)
    mask_rows = row_inside(count1, rows1, HALO1)
    for k in range(width1 // 256):
        at = slice(256 * k, 256 * k + 256)
        total = one[body1, at] + apply_rows(matrix, times(joined(even, odd, k), spread))
        one[body1, at] = jnp.where(mask_rows & inside1[:, at], total, 0.0)
    sweep(one, two, source1, gain1, rows1, HALO1, tiles1)
    sweep(two, one, source1, gain1, rows1, HALO1, tiles1)
    sweep(one, two, source1, gain1, rows1, HALO1, tiles1)

    rows, cols = image.shape
    width = wide_noisy.shape[1]
    count = rows + 2 * HALO0
    tiles = count // 8
    body0 = slice(GUARD, GUARD + count)
    inside = col_inside(width, cols, 64)
    gain = jnp.where(inside, 0.8 / centre(0), 0.0)
    mask_rows = row_inside(count, rows, HALO0)
    near1 = two[GUARD + HALO1 - 8 : GUARD + HALO1 - 8 + 144, :]
    matrix = spread_rows(count, 144, 4)
    even, odd = spread_cols(near1)

    def add(at, wide):
        total = values[body0, at] + apply_rows(matrix, wide)
        values[body0, at] = jnp.where(mask_rows & inside[:, at], total, 0.0)

    for k in range(cols // 256):
        add(slice(256 * k, 256 * k + 256), times(joined(even, odd, k), spread))
    lane = iota((1, 128), 1)
    last = [jnp.where(lane < 64, x[:, cols1 : cols1 + 128], x[:, cols1 + 128 : width1]) for x in (even, odd)]
    add(slice(cols, width), times(jnp.concatenate(last, axis=1), spread_tail))

    sweep(values, other, source, gain, rows, HALO0, tiles)
    sweep(other, values, source, gain, rows, HALO0, tiles)

    def last_sweep(tile, start):
        middle, near = neighbours(values, start)
        k = gain * tile_valid(tile, rows, HALO0)
        s = source[pl.ds(start + 8, 8), :]
        e = 0.2 * middle + k * (s + near)
        other[pl.ds(start + 8, 8), :] = e + (wide_noisy[pl.ds(start + 8, 8), :] + 0.25 * s)

    for_tiles(0, tiles, last_sweep)

    half_cols = half_cols_mask(width, cols, 64)

    def dual_step(tile, start):
        x = other[pl.ds(start + 8, 16), :]
        w = x[0:8]
        half_rows = 0.5 * dual_masks(tile, rows, width, cols, HALO0, 64)
        here = pl.ds(start + 8, 8)
        qa = dual_a[here, :] + half_rows * (x[1:9] - w)
        qb = dual_b[here, :] + half_cols * (east(w) - w)
        a, b = shrunk(qa, qb, wide_strength[here, :])
        new_a[here, :] = a
        return w, a, b

    dual_step(0, 0)

    def last_step(tile, start):
        w, a, b = dual_step(tile, start)
        above = new_a[pl.ds(start, 16), :][7:15]
        d = (a - above) + (b - west(b))
        out = pl.ds(pl.multiple_of(start - 8, 8), 8)
        noisy = wide_noisy[pl.ds(start + 8, 8), :]
        image[out, :] = (0.8 * w + 0.2 * (d + noisy))[:, 0:cols]
        dual[0, out, :] = a[:, 0:cols]
        dual[1, out, :] = b[:, 0:cols]

    for_tiles(1, tiles - 1, last_step, unroll=1)


def in_vmem(count):
    return [pl.BlockSpec(memory_space=VMEM)] * count


def shapes(*dims):
    return [jax.ShapeDtypeStruct(d, F32) for d in dims]


def from_directions(pieces):
    up_sent, down_sent, left_sent, right_sent, ul, ur, dl, dr = pieces
    return (down_sent, up_sent, right_sent, left_sent, dr, dl, ur, ul)


def per_device(noisy, strength):
    rows, cols = noisy.shape
    sems = [pltpu.SemaphoreType.DMA((8,)), pltpu.SemaphoreType.DMA((8,))]
    pieces = pl.pallas_call(
        exchange_image,
        out_shape=shapes(*[(16, cols)] * 2, *[(32, 128)] * 2, *[(16, 128)] * 4),
        in_specs=in_vmem(2),
        out_specs=in_vmem(8),
        scratch_shapes=[VMEM((2, 16, cols), F32), VMEM((2, 32, 128), F32), VMEM((4, 16, 128), F32)] + sems,
        compiler_params=pltpu.CompilerParams(
            collective_id=0, has_side_effects=True, vmem_limit_bytes=VMEM_LIMIT
        ),
    )(noisy, strength)
    wide = (rows + 2 * HALO0 + 2 * GUARD, cols + 128)
    rows1, cols1 = rows // 2, cols // 2
    *kept, coarse = pl.pallas_call(
        down_level0,
        out_shape=shapes(*[wide] * 6, (rows1, cols1)),
        in_specs=in_vmem(10),
        out_specs=in_vmem(7),
        scratch_shapes=[VMEM(wide, F32)],
        compiler_params=pltpu.CompilerParams(vmem_limit_bytes=VMEM_LIMIT),
    )(noisy, strength, *from_directions(pieces))
    pieces = pl.pallas_call(
        exchange_source,
        out_shape=shapes(
            *[(HALO1, cols1)] * 2, *[(rows1, 128)] * 2, *[(HALO1, 128)] * 4
        ),
        in_specs=in_vmem(1),
        out_specs=in_vmem(8),
        scratch_shapes=sems,
        compiler_params=pltpu.CompilerParams(
            collective_id=1, has_side_effects=True, vmem_limit_bytes=VMEM_LIMIT
        ),
    )(coarse)
    wide1 = (rows1 + 2 * HALO1 + 2 * GUARD, cols1 + 256)
    image, dual = pl.pallas_call(
        up_levels,
        out_shape=shapes((rows, cols), (2, rows, cols)),
        in_specs=in_vmem(15),
        out_specs=in_vmem(2),
        scratch_shapes=[VMEM(wide1, F32)] * 3 + [VMEM(wide, F32)] * 2,
        input_output_aliases={},
        compiler_params=pltpu.CompilerParams(vmem_limit_bytes=VMEM_LIMIT),
    )(coarse, *from_directions(pieces), *kept)
    return image, dual


def solution(mesh):
    placed = (P("row", "col"), P("row", "col"))
    return jax.shard_map(
        per_device,
        mesh=mesh,
        in_specs=placed,
        out_specs=(P("row", "col"), P(None, "row", "col")),
        check_vma=False,
    )
```

profile of v0, /device:TPU:11, one launch (start us, length us, event | category | flops | bytes accessed | tf_op | source)
XLA Modules:
  0.0 72.6 jit_solution(12132576752786046079)
XLA Ops:
  0.6 9.3 %shard_map.41 = (f32[16,1024]{1,0:T(8,128)}, f32[16,1024]{1,0:T(8,128)}, f32[32,128]{1,0:T(8,128)}, f32[32,128]{1,0:T(8,128)}, f32[16,128]{1,0:T(8,128)}, /*inde...) custom-call(f32[256,1024]{1,0:T(8,128)} %noisy.3, f32[256,1024]{1,0:T(8,128)} %strength.3), custom_call_target="tpu_custom_call" | custom-call | tf_op jit(solution)/shard_map/pallas_call | solution.py:584
  10.0 18.0 %shard_map.42 = (f32[288,1152]{1,0:T(8,128)}, f32[288,1152]{1,0:T(8,128)}, f32[288,1152]{1,0:T(8,128)}, f32[288,1152]{1,0:T(8,128)}, f32[288,1152]{1,0:T(8,128)}...) custom-call(f32[256,1024]{1,0:T(8,128)} %noisy.3, f32[256,1024]{1,0:T(8,128)} %strength.3, f32[16,1024]{1,0:T(8,128)} %get-tuple-element.25.up, ...), custom_call_target="tpu_custom_call" | custom-call | tf_op jit(solution)/shard_map/pallas_call | solution.py:596
  27.9 10.8 %shard_map.43 = (f32[72,512]{1,0:T(8,128)}, f32[72,512]{1,0:T(8,128)}, f32[128,128]{1,0:T(8,128)}, f32[128,128]{1,0:T(8,128)}, f32[72,128]{1,0:T(8,128)}, /*inde...) custom-call(f32[128,512]{1,0:T(8,128)} %get-tuple-element.33.source.coarse), custom_call_target="tpu_custom_call" | custom-call | tf_op jit(solution)/shard_map/pallas_call | solution.py:604
  38.7 33.9 %shard_map.44 = (f32[256,1024]{1,0:T(8,128)}, f32[2,256,1024]{2,1,0:T(8,128)}) custom-call(f32[128,512]{1,0:T(8,128)} %get-tuple-element.33.source.coarse, f32[72,512]{1,0:T(8,128)} %get-tuple-element.34.up, f32[72,512]{1,0:T(8,128)} %get-tuple-element.35.down, f32[128,128]{1,0:T(8,128)} %get-tuple-element.36.left, f32[128,128]{1,0:T(8,128)} %get-tuple-element.37.right, ...), custom_call_target="tpu_custom_call" | custom-call | tf_op jit(solution)/shard_map/pallas_call | solution.py:617
where the time goes:
time: 72.8 us; the launch traced here: 72.6 us
  Pallas kernels  72 us (99%)
    pallas_call x1, Pallas kernels, per_device(): pl.pallas_call(up_levels, out_shape=shapes((rows, cols), (2, rows, cols))...  33.9 us
    pallas_call x1, Pallas kernels, per_device(): pl.pallas_call(down_level0, out_shape=shapes(*[wide] * 6, (rows1, cols1))...  18 us
    pallas_call x1, Pallas kernels, per_device(): pl.pallas_call(exchange_source, out_shape=shapes(*[(HALO1, cols1)] * 2, *...  10.8 us
    pallas_call x1, Pallas kernels, per_device(): pl.pallas_call(exchange_image, out_shape=shapes(*[(16, cols)] * 2, *[(32,...  9.32 us

commit v1 on v0

--- a/solution.py
+++ b/solution.py
@@ -16,6 +16,7 @@
 GUARD = 8
 HALO0 = 8
 HALO1 = 72
+CHUNK = 16
 DIRECTIONS = ((-1, 0), (1, 0), (0, -1), (0, 1), (-1, -1), (-1, 1), (1, -1), (1, 1))
 VMEM_LIMIT = 58 * 1024 * 1024
 
@@ -243,39 +244,51 @@
     return jnp.where((g >= 0) & (g < own * lax.axis_size("row")), 1.0, 0.0)
 
 
+def chunk_gain(gain, tile, own, halo):
+    wide = jnp.broadcast_to(gain, (8, gain.shape[1]))
+    return jnp.concatenate(
+        [wide * tile_valid(tile + k, own, halo) for k in range(CHUNK // 8)], axis=0
+    )
+
+
 def neighbours(ref, start):
-    x = ref[pl.ds(start, 24), :]
-    middle = x[8:16]
-    return middle, (x[7:15] + x[9:17]) + (west(middle) + east(middle))
-
-
-def for_tiles(first, last, body, unroll=2):
-    def step(tile, carry):
+    x = ref[pl.ds(start, CHUNK + 16), :]
+    middle = x[8 : CHUNK + 8]
+    return middle, (x[7 : CHUNK + 7] + x[9 : CHUNK + 9]) + (west(middle) + east(middle))
+
+
+def for_chunks(first, tiles, body, unroll=1):
+    def step(chunk, carry):
+        tile = first + chunk * (CHUNK // 8)
         body(tile, pl.multiple_of(tile * 8, 8))
         return carry
 
-    lax.fori_loop(first, last, step, 0, unroll=unroll)
-
-
-def sweep(old, new, source, gain, own, halo, tiles):
+    lax.fori_loop(0, tiles * 8 // CHUNK, step, 0, unroll=unroll)
+
+
+def inner(start):
+    return pl.ds(start + 8, CHUNK)
+
+
+def sweep(old, new, source, gain, own, halo, first, tiles):
     def body(tile, start):
         middle, beside = neighbours(old, start)
-        k = gain * tile_valid(tile, own, halo)
-        new[pl.ds(start + 8, 8), :] = 0.2 * middle + k * (source[pl.ds(start + 8, 8), :] + beside)
-
-    for_tiles(0, tiles, body)
+        k = chunk_gain(gain, tile, own, halo)
+        new[inner(start), :] = 0.2 * middle + k * (source[inner(start), :] + beside)
+
+    for_chunks(first, tiles, body)
 
 
 def first_sweep(new, source, gain, own, halo, tiles):
     def body(tile, start):
-        k = gain * tile_valid(tile, own, halo)
-        new[pl.ds(start + 8, 8), :] = k * source[pl.ds(start + 8, 8), :]
-
-    for_tiles(0, tiles, body)
-
-
-def dual_masks(tile, own_rows, width, own_cols, halo, right):
-    g = lax.axis_index("row") * own_rows - halo + tile * 8 + iota((8, 1), 0)
+        k = chunk_gain(gain, tile, own, halo)
+        new[inner(start), :] = k * source[inner(start), :]
+
+    for_chunks(0, tiles, body)
+
+
+def dual_masks(tile, count, own_rows, halo):
+    g = lax.axis_index("row") * own_rows - halo + tile * 8 + iota((count, 1), 0)
     return jnp.where((g >= 0) & (g < own_rows * lax.axis_size("row") - 1), 1.0, 0.0)
 
 
@@ -344,42 +357,36 @@
     half_cols = half_cols_mask(width, cols, 64)
 
     def first_step(tile, start):
-        x = wide_noisy[pl.ds(start + 8, 16), :]
-        w = x[0:8]
-        half_rows = 0.5 * dual_masks(tile, rows, width, cols, HALO0, 64)
-        qa = half_rows * (x[1:9] - w)
+        x = wide_noisy[pl.ds(start + 8, CHUNK + 8), :]
+        w = x[0:CHUNK]
+        half_rows = 0.5 * dual_masks(tile, CHUNK, rows, HALO0)
+        qa = half_rows * (x[1 : CHUNK + 1] - w)
         qb = half_cols * (east(w) - w)
-        a, b = shrunk(qa, qb, wide_strength[pl.ds(start + 8, 8), :])
-        dual_a[pl.ds(start + 8, 8), :] = a
-        dual_b[pl.ds(start + 8, 8), :] = b
-        above = dual_a[pl.ds(start, 16), :][7:15]
+        before = dual_a[pl.ds(start, 8), :]
+        a, b = shrunk(qa, qb, wide_strength[inner(start), :])
+        dual_a[inner(start), :] = a
+        dual_b[inner(start), :] = b
+        above = jnp.concatenate([before, a], axis=0)[7 : CHUNK + 7]
         s = 0.8 * ((a - above) + (b - west(b)))
-        source[pl.ds(start + 8, 8), :] = s
-        other[pl.ds(start + 8, 8), :] = (gain * tile_valid(tile, rows, HALO0)) * s
-
-    for_tiles(0, tiles, first_step, unroll=1)
-    sweep(other, values, source, gain, rows, HALO0, tiles)
-    sweep(values, other, source, gain, rows, HALO0, tiles)
+        source[inner(start), :] = s
+        values[inner(start), :] = chunk_gain(gain, tile, rows, HALO0) * s
+
+    for_chunks(0, tiles, first_step)
+    sweep(values, other, source, gain, rows, HALO0, 0, tiles)
+    sweep(other, values, source, gain, rows, HALO0, 0, tiles)
 
     def residual(tile, start):
-        middle, beside = neighbours(other, start)
-        values[pl.ds(start + 8, 8), :] = (
-            source[pl.ds(start + 8, 8), :] - centre(0) * middle + beside
-        )
-
-    for_tiles(1, tiles - 1, residual)
+        middle, beside = neighbours(values, start)
+        other[inner(start), :] = source[inner(start), :] - centre(0) * middle + beside
+
+    for_chunks(1, tiles - 2, residual)
     rows_matrix = pair_rows(rows // 2, rows)
     cols_matrix = pair_cols()
     for block in range(cols // 256):
-        piece = values[top : top + rows, 256 * block : 256 * block + 256]
+        piece = other[top : top + rows, 256 * block : 256 * block + 256]
         coarse[:, 128 * block : 128 * block + 128] = times(
             apply_rows(rows_matrix, piece), cols_matrix
         )
-
-    def back(tile, start):
-        values[pl.ds(start + 8, 8), :] = other[pl.ds(start + 8, 8), :]
-
-    for_tiles(0, tiles, back)
 
 
 def relax(e, source, gain):
@@ -425,7 +432,9 @@
     wide = jnp.concatenate(
         [times(joined(even, odd, 0), spread), times(joined(even, odd, 1), spread_tail)], axis=1
     )
-    e2 = e2 + apply_rows(spread_rows(n2, n3, 0), wide)
+    kept = slice(24, 120)
+    e2, source2, gain2 = e2[kept], source2[kept], gain2[kept]
+    e2 = e2 + apply_rows(spread_rows(96, n3, 12), wide)
     e2 = jnp.where(gain2 > 0.0, e2, 0.0)
     for _ in range(3):
         e2 = relax(e2, source2, gain2)
@@ -434,10 +443,16 @@
 
 def up_levels(
     coarse, up, down, left, right, upleft, upright, downleft, downright,
-    wide_noisy, wide_strength, dual_a, dual_b, source, values,
-    image, dual,
-    source1, one, two, other, new_a,
+    *rest,
 ):
+    far, (image, dual), local = rest[:6], rest[6:8], rest[8:14]
+    source1, one, two, other, new_a, fetched = rest[14:]
+    wide_noisy, wide_strength, dual_a, dual_b, source, values = local
+    copies = [
+        pltpu.make_async_copy(far[k], local[k], fetched.at[k]) for k in range(len(far))
+    ]
+    for copy in copies:
+        copy.start()
     rows1, cols1 = coarse.shape
     width1 = cols1 + 256
     tiles1 = (source1.shape[0] - 2 * GUARD) // 8
@@ -470,14 +485,14 @@
     inside1 = col_inside(width1, cols1, 128)
     gain1 = jnp.where(inside1, 0.8 / centre(1), 0.0)
     first_sweep(one, source1, gain1, rows1, HALO1, tiles1)
-    sweep(one, two, source1, gain1, rows1, HALO1, tiles1)
-    sweep(two, one, source1, gain1, rows1, HALO1, tiles1)
+    sweep(one, two, source1, gain1, rows1, HALO1, 0, tiles1)
+    sweep(two, one, source1, gain1, rows1, HALO1, 0, tiles1)
 
     def residual(tile, start):
         middle, near = neighbours(one, start)
-        two[pl.ds(start + 8, 8), :] = source1[pl.ds(start + 8, 8), :] - centre(1) * middle + near
-
-    for_tiles(0, tiles1, residual)
+        two[inner(start), :] = source1[inner(start), :] - centre(1) * middle + near
+
+    for_chunks(0, tiles1, residual)
     count1 = 8 * tiles1
     body1 = slice(GUARD, GUARD + count1)
     rows_matrix = pair_rows(144, count1)
@@ -492,17 +507,22 @@
     e2 = coarse_levels(source2, rows1 // 2, cols1 // 2)
 
     spread, spread_tail = interleave(), interleave_tail()
-    matrix = spread_rows(count1, 144, 0)
+    near_first = (HALO1 - 8) // 8
+    near_count = rows1 + 16
+    near_rows = slice(GUARD + HALO1 - 8, GUARD + HALO1 - 8 + near_count)
+    matrix = spread_rows(near_count, 96, 8)
     even, odd = spread_cols(e2)
-    mask_rows = row_inside(count1, rows1, HALO1)
+    mask_rows = row_inside(near_count, rows1, 8)
     for k in range(width1 // 256):
         at = slice(256 * k, 256 * k + 256)
-        total = one[body1, at] + apply_rows(matrix, times(joined(even, odd, k), spread))
-        one[body1, at] = jnp.where(mask_rows & inside1[:, at], total, 0.0)
-    sweep(one, two, source1, gain1, rows1, HALO1, tiles1)
-    sweep(two, one, source1, gain1, rows1, HALO1, tiles1)
-    sweep(one, two, source1, gain1, rows1, HALO1, tiles1)
-
+        total = one[near_rows, at] + apply_rows(matrix, times(joined(even, odd, k), spread))
+        one[near_rows, at] = jnp.where(mask_rows & inside1[:, at], total, 0.0)
+    sweep(one, two, source1, gain1, rows1, HALO1, near_first, near_count // 8)
+    sweep(two, one, source1, gain1, rows1, HALO1, near_first, near_count // 8)
+    sweep(one, two, source1, gain1, rows1, HALO1, near_first, near_count // 8)
+
+    for copy in copies:
+        copy.wait()
     rows, cols = image.shape
     width = wide_noisy.shape[1]
     count = rows + 2 * HALO0
@@ -511,8 +531,8 @@
     inside = col_inside(width, cols, 64)
     gain = jnp.where(inside, 0.8 / centre(0), 0.0)
     mask_rows = row_inside(count, rows, HALO0)
-    near1 = two[GUARD + HALO1 - 8 : GUARD + HALO1 - 8 + 144, :]
-    matrix = spread_rows(count, 144, 4)
+    near1 = two[near_rows, :]
+    matrix = spread_rows(count, near_count, 4)
     even, odd = spread_cols(near1)
 
     def add(at, wide):
@@ -525,44 +545,45 @@
     last = [jnp.where(lane < 64, x[:, cols1 : cols1 + 128], x[:, cols1 + 128 : width1]) for x in (even, odd)]
     add(slice(cols, width), times(jnp.concatenate(last, axis=1), spread_tail))
 
-    sweep(values, other, source, gain, rows, HALO0, tiles)
-    sweep(other, values, source, gain, rows, HALO0, tiles)
+    sweep(values, other, source, gain, rows, HALO0, 0, tiles)
+    sweep(other, values, source, gain, rows, HALO0, 0, tiles)
 
     def last_sweep(tile, start):
         middle, near = neighbours(values, start)
-        k = gain * tile_valid(tile, rows, HALO0)
-        s = source[pl.ds(start + 8, 8), :]
+        k = chunk_gain(gain, tile, rows, HALO0)
+        s = source[inner(start), :]
         e = 0.2 * middle + k * (s + near)
-        other[pl.ds(start + 8, 8), :] = e + (wide_noisy[pl.ds(start + 8, 8), :] + 0.25 * s)
-
-    for_tiles(0, tiles, last_sweep)
+        other[inner(start), :] = e + (wide_noisy[inner(start), :] + 0.25 * s)
+
+    for_chunks(0, tiles, last_sweep)
 
     half_cols = half_cols_mask(width, cols, 64)
 
-    def dual_step(tile, start):
-        x = other[pl.ds(start + 8, 16), :]
-        w = x[0:8]
-        half_rows = 0.5 * dual_masks(tile, rows, width, cols, HALO0, 64)
-        here = pl.ds(start + 8, 8)
-        qa = dual_a[here, :] + half_rows * (x[1:9] - w)
+    def dual_step(tile, start, size):
+        x = other[pl.ds(start + 8, size + 8), :]
+        w = x[0:size]
+        half_rows = 0.5 * dual_masks(tile, size, rows, HALO0)
+        here = pl.ds(start + 8, size)
+        qa = dual_a[here, :] + half_rows * (x[1 : size + 1] - w)
         qb = dual_b[here, :] + half_cols * (east(w) - w)
         a, b = shrunk(qa, qb, wide_strength[here, :])
-        new_a[here, :] = a
         return w, a, b
 
-    dual_step(0, 0)
+    new_a[8:16, :] = dual_step(0, 0, 8)[1]
 
     def last_step(tile, start):
-        w, a, b = dual_step(tile, start)
-        above = new_a[pl.ds(start, 16), :][7:15]
+        before = new_a[pl.ds(start, 8), :]
+        w, a, b = dual_step(tile, start, CHUNK)
+        new_a[inner(start), :] = a
+        above = jnp.concatenate([before, a], axis=0)[7 : CHUNK + 7]
         d = (a - above) + (b - west(b))
-        out = pl.ds(pl.multiple_of(start - 8, 8), 8)
-        noisy = wide_noisy[pl.ds(start + 8, 8), :]
+        out = pl.ds(pl.multiple_of(start - 8, 8), CHUNK)
+        noisy = wide_noisy[inner(start), :]
         image[out, :] = (0.8 * w + 0.2 * (d + noisy))[:, 0:cols]
         dual[0, out, :] = a[:, 0:cols]
         dual[1, out, :] = b[:, 0:cols]
 
-    for_tiles(1, tiles - 1, last_step, unroll=1)
+    for_chunks(1, tiles - 2, last_step)
 
 
 def in_vmem(count):
@@ -617,10 +638,12 @@
     image, dual = pl.pallas_call(
         up_levels,
         out_shape=shapes((rows, cols), (2, rows, cols)),
-        in_specs=in_vmem(15),
+        in_specs=in_vmem(9) + [pl.BlockSpec(memory_space=pl.ANY)] * 6,
         out_specs=in_vmem(2),
-        scratch_shapes=[VMEM(wide1, F32)] * 3 + [VMEM(wide, F32)] * 2,
-        input_output_aliases={},
+        scratch_shapes=[VMEM(wide, F32)] * 6
+        + [VMEM(wide1, F32)] * 3
+        + [VMEM(wide, F32)] * 2
+        + [pltpu.SemaphoreType.DMA((6,))],
         compiler_params=pltpu.CompilerParams(vmem_limit_bytes=VMEM_LIMIT),
     )(coarse, *from_directions(pieces), *kept)
     return image, dual

time: 72.8 us -> 62.1 us (0.85)
  Pallas kernels: 72 us -> 61.2 us
    pallas_call x1, Pallas kernels: 33.9 us -> 26.7 us  [per_device(): pl.pallas_call(up_levels, out_shape=shapes((rows, cols), (2, rows, cols))...]
    pallas_call x1, Pallas kernels: 18 us -> 14.4 us  [per_device(): pl.pallas_call(down_level0, out_shape=shapes(*[wide] * 6, (rows1, cols1))...]
where the time goes in v1:
time: 62.1 us; the launch traced here: 61.9 us
  Pallas kernels  61.2 us (99%)
  between operations  0.65 us (1%)
    pallas_call x1, Pallas kernels, per_device(): pl.pallas_call(up_levels, out_shape=shapes((rows, cols), (2, rows, cols))...  26.7 us
    pallas_call x1, Pallas kernels, per_device(): pl.pallas_call(down_level0, out_shape=shapes(*[wide] * 6, (rows1, cols1))...  14.4 us
    pallas_call x1, Pallas kernels, per_device(): pl.pallas_call(exchange_source, out_shape=shapes(*[(HALO1, cols1)] * 2, *...  10.8 us
    pallas_call x1, Pallas kernels, per_device(): pl.pallas_call(exchange_image, out_shape=shapes(*[(16, cols)] * 2, *[(32,...  9.32 us

profile of v1, /device:TPU:11, one launch (start us, length us, event | category | flops | bytes accessed | tf_op | source)
XLA Modules:
  0.0 61.9 jit_solution(15481444008917193346)
XLA Ops:
  0.6 9.3 %shard_map.41 = (f32[16,1024]{1,0:T(8,128)}, f32[16,1024]{1,0:T(8,128)}, f32[32,128]{1,0:T(8,128)}, f32[32,128]{1,0:T(8,128)}, f32[16,128]{1,0:T(8,128)}, /*inde...) custom-call(f32[256,1024]{1,0:T(8,128)} %noisy.3, f32[256,1024]{1,0:T(8,128)} %strength.3), custom_call_target="tpu_custom_call" | custom-call | tf_op jit(solution)/shard_map/pallas_call | solution.py:605
  10.0 14.4 %shard_map.42 = (f32[288,1152]{1,0:T(8,128)}, f32[288,1152]{1,0:T(8,128)}, f32[288,1152]{1,0:T(8,128)}, f32[288,1152]{1,0:T(8,128)}, f32[288,1152]{1,0:T(8,128)}...) custom-call(f32[256,1024]{1,0:T(8,128)} %noisy.3, f32[256,1024]{1,0:T(8,128)} %strength.3, f32[16,1024]{1,0:T(8,128)} %get-tuple-element.25.up, ...), custom_call_target="tpu_custom_call" | custom-call | tf_op jit(solution)/shard_map/pallas_call | solution.py:617
  24.4 10.8 %shard_map.43 = (f32[72,512]{1,0:T(8,128)}, f32[72,512]{1,0:T(8,128)}, f32[128,128]{1,0:T(8,128)}, f32[128,128]{1,0:T(8,128)}, f32[72,128]{1,0:T(8,128)}, /*inde...) custom-call(f32[128,512]{1,0:T(8,128)} %get-tuple-element.33.source.coarse), custom_call_target="tpu_custom_call" | custom-call | tf_op jit(solution)/shard_map/pallas_call | solution.py:625
  35.2 26.7 %shard_map.44 = (f32[256,1024]{1,0:T(8,128)}, f32[2,256,1024]{2,1,0:T(8,128)}) custom-call(f32[128,512]{1,0:T(8,128)} %get-tuple-element.33.source.coarse, f32[72,512]{1,0:T(8,128)} %get-tuple-element.34.up, f32[72,512]{1,0:T(8,128)} %get-tuple-element.35.down, f32[128,128]{1,0:T(8,128)} %get-tuple-element.36.left, f32[128,128]{1,0:T(8,128)} %get-tuple-element.37.right, ...), custom_call_target="tpu_custom_call" | custom-call | tf_op jit(solution)/shard_map/pallas_call | solution.py:638

commit v2 on v1

--- a/solution.py
+++ b/solution.py
@@ -257,7 +257,7 @@
     return middle, (x[7 : CHUNK + 7] + x[9 : CHUNK + 9]) + (west(middle) + east(middle))
 
 
-def for_chunks(first, tiles, body, unroll=1):
+def for_chunks(first, tiles, body, unroll=2):
     def step(chunk, carry):
         tile = first + chunk * (CHUNK // 8)
         body(tile, pl.multiple_of(tile * 8, 8))
@@ -310,8 +310,13 @@
 
 def down_level0(
     noisy, strength, up, down, left, right, upleft, upright, downleft, downright,
-    wide_noisy, wide_strength, dual_a, dual_b, source, values, coarse, other,
+    *rest,
 ):
+    far, coarse, local, (other, written) = rest[:6], rest[6], rest[7:13], rest[13:]
+    wide_noisy, wide_strength, dual_a, dual_b, source, values = local
+    copies = [
+        pltpu.make_async_copy(local[k], far[k], written.at[k]) for k in range(len(far))
+    ]
     rows, cols = noisy.shape
     width = wide_noisy.shape[1]
     total = wide_noisy.shape[0]
@@ -371,9 +376,15 @@
         source[inner(start), :] = s
         values[inner(start), :] = chunk_gain(gain, tile, rows, HALO0) * s
 
+    copies[0].start()
+    copies[1].start()
     for_chunks(0, tiles, first_step)
+    for copy in copies[2:5]:
+        copy.start()
     sweep(values, other, source, gain, rows, HALO0, 0, tiles)
     sweep(other, values, source, gain, rows, HALO0, 0, tiles)
+
+    copies[5].start()
 
     def residual(tile, start):
         middle, beside = neighbours(values, start)
@@ -387,6 +398,8 @@
         coarse[:, 128 * block : 128 * block + 128] = times(
             apply_rows(rows_matrix, piece), cols_matrix
         )
+    for copy in copies:
+        copy.wait()
 
 
 def relax(e, source, gain):
@@ -445,8 +458,8 @@
     coarse, up, down, left, right, upleft, upright, downleft, downright,
     *rest,
 ):
-    far, (image, dual), local = rest[:6], rest[6:8], rest[8:14]
-    source1, one, two, other, new_a, fetched = rest[14:]
+    far, (image_out, dual_out), local = rest[:6], rest[6:8], rest[8:14]
+    source1, one, two, other, new_a, image, dual, fetched, written = rest[14:]
     wide_noisy, wide_strength, dual_a, dual_b, source, values = local
     copies = [
         pltpu.make_async_copy(far[k], local[k], fetched.at[k]) for k in range(len(far))
@@ -583,7 +596,25 @@
         dual[0, out, :] = a[:, 0:cols]
         dual[1, out, :] = b[:, 0:cols]
 
-    for_chunks(1, tiles - 2, last_step)
+    parts = written.shape[0]
+    size = rows // parts
+    sent = []
+    for k in range(parts):
+        for_chunks(1 + k * size // 8, size // 8, last_step)
+        at = pl.ds(k * size, size)
+        sent.append(
+            pltpu.make_async_copy(image.at[at, :], image_out.at[at, :], written.at[k, 0])
+        )
+        for c in range(2):
+            sent.append(
+                pltpu.make_async_copy(
+                    dual.at[c, at, :], dual_out.at[c, at, :], written.at[k, 1 + c]
+                )
+            )
+        for copy in sent[-3:]:
+            copy.start()
+    for copy in sent:
+        copy.wait()
 
 
 def in_vmem(count):
@@ -618,8 +649,8 @@
         down_level0,
         out_shape=shapes(*[wide] * 6, (rows1, cols1)),
         in_specs=in_vmem(10),
-        out_specs=in_vmem(7),
-        scratch_shapes=[VMEM(wide, F32)],
+        out_specs=[pl.BlockSpec(memory_space=pl.ANY)] * 6 + in_vmem(1),
+        scratch_shapes=[VMEM(wide, F32)] * 7 + [pltpu.SemaphoreType.DMA((6,))],
         compiler_params=pltpu.CompilerParams(vmem_limit_bytes=VMEM_LIMIT),
     )(noisy, strength, *from_directions(pieces))
     pieces = pl.pallas_call(
@@ -639,11 +670,12 @@
         up_levels,
         out_shape=shapes((rows, cols), (2, rows, cols)),
         in_specs=in_vmem(9) + [pl.BlockSpec(memory_space=pl.ANY)] * 6,
-        out_specs=in_vmem(2),
+        out_specs=[pl.BlockSpec(memory_space=pl.ANY)] * 2,
         scratch_shapes=[VMEM(wide, F32)] * 6
         + [VMEM(wide1, F32)] * 3
         + [VMEM(wide, F32)] * 2
-        + [pltpu.SemaphoreType.DMA((6,))],
+        + [VMEM((rows, cols), F32), VMEM((2, rows, cols), F32)]
+        + [pltpu.SemaphoreType.DMA((6,)), pltpu.SemaphoreType.DMA((4, 3))],
         compiler_params=pltpu.CompilerParams(vmem_limit_bytes=VMEM_LIMIT),
     )(coarse, *from_directions(pieces), *kept)
     return image, dual

time: 62.1 us -> 50.7 us (0.82)
  Pallas kernels: 61.2 us -> 49.8 us
    pallas_call x1, Pallas kernels: 26.7 us -> 20.1 us  [per_device(): pl.pallas_call(up_levels, out_shape=shapes((rows, cols), (2, rows, cols))...]
    pallas_call x1, Pallas kernels: 14.4 us -> 9.57 us  [per_device(): pl.pallas_call(down_level0, out_shape=shapes(*[wide] * 6, (rows1, cols1))...]
where the time goes in v2:
time: 50.7 us; the launch traced here: 50.4 us
  Pallas kernels  49.8 us (98%)
  between operations  0.65 us (1%)
    pallas_call x1, Pallas kernels, per_device(): pl.pallas_call(up_levels, out_shape=shapes((rows, cols), (2, rows, cols))...  20.1 us
    pallas_call x1, Pallas kernels, per_device(): pl.pallas_call(exchange_source, out_shape=shapes(*[(HALO1, cols1)] * 2, *...  10.8 us
    pallas_call x1, Pallas kernels, per_device(): pl.pallas_call(down_level0, out_shape=shapes(*[wide] * 6, (rows1, cols1))...  9.57 us
    pallas_call x1, Pallas kernels, per_device(): pl.pallas_call(exchange_image, out_shape=shapes(*[(16, cols)] * 2, *[(32,...  9.32 us

profile of v2, /device:TPU:11, one launch (start us, length us, event | category | flops | bytes accessed | tf_op | source)
XLA Modules:
  0.0 50.4 jit_solution(17362506602251792763)
XLA Ops:
  0.6 9.3 %shard_map.41 = (f32[16,1024]{1,0:T(8,128)}, f32[16,1024]{1,0:T(8,128)}, f32[32,128]{1,0:T(8,128)}, f32[32,128]{1,0:T(8,128)}, f32[16,128]{1,0:T(8,128)}, /*inde...) custom-call(f32[256,1024]{1,0:T(8,128)} %noisy.3, f32[256,1024]{1,0:T(8,128)} %strength.3), custom_call_target="tpu_custom_call" | custom-call | tf_op jit(solution)/shard_map/pallas_call | solution.py:636
  10.0 9.6 %shard_map.42 = (f32[288,1152]{1,0:T(8,128)}, f32[288,1152]{1,0:T(8,128)}, f32[288,1152]{1,0:T(8,128)}, f32[288,1152]{1,0:T(8,128)}, f32[288,1152]{1,0:T(8,128)}...) custom-call(f32[256,1024]{1,0:T(8,128)} %noisy.3, f32[256,1024]{1,0:T(8,128)} %strength.3, f32[16,1024]{1,0:T(8,128)} %get-tuple-element.25.up, ...), custom_call_target="tpu_custom_call" | custom-call | tf_op jit(solution)/shard_map/pallas_call | solution.py:648
  19.5 10.8 %shard_map.43 = (f32[72,512]{1,0:T(8,128)}, f32[72,512]{1,0:T(8,128)}, f32[128,128]{1,0:T(8,128)}, f32[128,128]{1,0:T(8,128)}, f32[72,128]{1,0:T(8,128)}, /*inde...) custom-call(f32[128,512]{1,0:T(8,128)} %get-tuple-element.33.source.coarse), custom_call_target="tpu_custom_call" | custom-call | tf_op jit(solution)/shard_map/pallas_call | solution.py:656
  30.3 20.1 %shard_map.44 = (f32[256,1024]{1,0:T(8,128)}, f32[2,256,1024]{2,1,0:T(8,128)}) custom-call(f32[128,512]{1,0:T(8,128)} %get-tuple-element.33.source.coarse, f32[72,512]{1,0:T(8,128)} %get-tuple-element.34.up, f32[72,512]{1,0:T(8,128)} %get-tuple-element.35.down, f32[128,128]{1,0:T(8,128)} %get-tuple-element.36.left, f32[128,128]{1,0:T(8,128)} %get-tuple-element.37.right, ...), custom_call_target="tpu_custom_call" | custom-call | tf_op jit(solution)/shard_map/pallas_call | solution.py:669

commit v3 on v2

--- a/solution.py
+++ b/solution.py
@@ -257,7 +257,7 @@
     return middle, (x[7 : CHUNK + 7] + x[9 : CHUNK + 9]) + (west(middle) + east(middle))
 
 
-def for_chunks(first, tiles, body, unroll=2):
+def for_chunks(first, tiles, body, unroll=4):
     def step(chunk, carry):
         tile = first + chunk * (CHUNK // 8)
         body(tile, pl.multiple_of(tile * 8, 8))

time: 50.7 us -> 47 us (0.927)
  Pallas kernels: 49.8 us -> 46.1 us
    pallas_call x1, Pallas kernels: 20.1 us -> 17.6 us  [per_device(): pl.pallas_call(up_levels, out_shape=shapes((rows, cols), (2, rows, cols))...]
    pallas_call x1, Pallas kernels: 9.57 us -> 8.4 us  [per_device(): pl.pallas_call(down_level0, out_shape=shapes(*[wide] * 6, (rows1, cols1))...]
where the time goes in v3:
time: 47 us; the launch traced here: 46.7 us
  Pallas kernels  46.1 us (98%)
  between operations  0.65 us (1%)
    pallas_call x1, Pallas kernels, per_device(): pl.pallas_call(up_levels, out_shape=shapes((rows, cols), (2, rows, cols))...  17.6 us
    pallas_call x1, Pallas kernels, per_device(): pl.pallas_call(exchange_source, out_shape=shapes(*[(HALO1, cols1)] * 2, *...  10.8 us
    pallas_call x1, Pallas kernels, per_device(): pl.pallas_call(exchange_image, out_shape=shapes(*[(16, cols)] * 2, *[(32,...  9.32 us
    pallas_call x1, Pallas kernels, per_device(): pl.pallas_call(down_level0, out_shape=shapes(*[wide] * 6, (rows1, cols1))...  8.4 us

profile of v3, /device:TPU:11, one launch (start us, length us, event | category | flops | bytes accessed | tf_op | source)
XLA Modules:
  0.0 46.7 jit_solution(585594919876717734)
XLA Ops:
  0.6 9.3 %shard_map.41 = (f32[16,1024]{1,0:T(8,128)}, f32[16,1024]{1,0:T(8,128)}, f32[32,128]{1,0:T(8,128)}, f32[32,128]{1,0:T(8,128)}, f32[16,128]{1,0:T(8,128)}, /*inde...) custom-call(f32[256,1024]{1,0:T(8,128)} %noisy.3, f32[256,1024]{1,0:T(8,128)} %strength.3), custom_call_target="tpu_custom_call" | custom-call | tf_op jit(solution)/shard_map/pallas_call | solution.py:636
  10.0 8.4 %shard_map.42 = (f32[288,1152]{1,0:T(8,128)}, f32[288,1152]{1,0:T(8,128)}, f32[288,1152]{1,0:T(8,128)}, f32[288,1152]{1,0:T(8,128)}, f32[288,1152]{1,0:T(8,128)}...) custom-call(f32[256,1024]{1,0:T(8,128)} %noisy.3, f32[256,1024]{1,0:T(8,128)} %strength.3, f32[16,1024]{1,0:T(8,128)} %get-tuple-element.25.up, ...), custom_call_target="tpu_custom_call" | custom-call | tf_op jit(solution)/shard_map/pallas_call | solution.py:648
  18.4 10.8 %shard_map.43 = (f32[72,512]{1,0:T(8,128)}, f32[72,512]{1,0:T(8,128)}, f32[128,128]{1,0:T(8,128)}, f32[128,128]{1,0:T(8,128)}, f32[72,128]{1,0:T(8,128)}, /*inde...) custom-call(f32[128,512]{1,0:T(8,128)} %get-tuple-element.33.source.coarse), custom_call_target="tpu_custom_call" | custom-call | tf_op jit(solution)/shard_map/pallas_call | solution.py:656
  29.2 17.6 %shard_map.44 = (f32[256,1024]{1,0:T(8,128)}, f32[2,256,1024]{2,1,0:T(8,128)}) custom-call(f32[128,512]{1,0:T(8,128)} %get-tuple-element.33.source.coarse, f32[72,512]{1,0:T(8,128)} %get-tuple-element.34.up, f32[72,512]{1,0:T(8,128)} %get-tuple-element.35.down, f32[128,128]{1,0:T(8,128)} %get-tuple-element.36.left, f32[128,128]{1,0:T(8,128)} %get-tuple-element.37.right, ...), custom_call_target="tpu_custom_call" | custom-call | tf_op jit(solution)/shard_map/pallas_call | solution.py:669
